TPU v7x, 32 devices: a whole 2x2x4 slice. The times are simulated.
32 devices in a mesh: dp: 4 (over y, core), graph: 8 (over z, x).
Axes of the slice: x: 2, y: 2, z: 4, core: 2. Of those that a mesh axis runs over, the one named last changes fastest.
Arguments:
- node_features: bfloat16 [128, 49, 128], P(('dp', 'graph')), may hold values from -6 to 6
- cotangent: bfloat16 [128, 49, 128], P(('dp', 'graph')), may hold values from -0.59765625 to 0.59765625
- wigner: float32 [235, 4096], P(None, ('dp', 'graph')), may hold values from -2.4 to 2.4
- w_zero: bfloat16 [896, 896], replicated, may hold values from -0.1875 to 0.1875
- w_one_re: bfloat16 [768, 768], replicated, may hold values from -0.15625 to 0.15625
- w_one_im: bfloat16 [768, 768], replicated, may hold values from -0.15625 to 0.15625
- w_two_re: bfloat16 [640, 640], replicated, may hold values from -0.15625 to 0.15625
- w_two_im: bfloat16 [640, 640], replicated, may hold values from -0.15625 to 0.15625
- w_attn: bfloat16 [896, 8], replicated, may hold values from -0.1875 to 0.1875
- src_slot: int32 [4096], P(('dp', 'graph')), may hold values from 0 to 15
- dst_node: int32 [4096], P(('dp', 'graph')), may hold values from 0 to 3
- request: int32 [32, 8, 2], P(('dp', 'graph')), may hold values from 0 to 3, as said below
- edge_count: int32 [32], P(('dp', 'graph')), may hold values from 1 to 128, 2560 in all
Outputs:
- node_grad: float32 [128, 49, 128], P(('dp', 'graph'))
- grad_zero: float32 [896, 896], P('graph')
- grad_one_re: float32 [768, 768], P('graph')
- grad_one_im: float32 [768, 768], P('graph')
- grad_two_re: float32 [640, 640], P('graph')
- grad_two_im: float32 [640, 640], P('graph')
- grad_attn: float32 [896, 8], P('graph')
Inputs may be any that keep to these rules, and one draw needn't show every extreme that they name: request[k, p] holds 2 distinct nodes, numbered within device p of device k's data group, that device k reads from device p. The first edge_count[k] edges of device k are live and the rest are padding; some device has 128.
All inputs are finite; a program needn't handle non-finite values.
Results may differ from a plain program's by a relative error of at most 0.014.
Values may be sent and summed in bfloat16 or wider, within the bound.
A program may use at most 128 MiB of HBM per device.

v0:
```python
import functools

import jax
import jax.numpy as jnp
from jax import lax
from jax.experimental import pallas as pl
from jax.experimental.pallas import tpu as pltpu
from jax.sharding import PartitionSpec as P

LMAX = 6
MMAX = 2
NCOEF = (LMAX + 1) ** 2
ORDERS = (0, 1, -1, 2, -2)
MESH = pl.DeviceIdType.MESH
BF = jnp.bfloat16
F32 = jnp.float32
QUARTERS = 4
WIDTH = -(-NCOEF // QUARTERS)
CHUNK = 32


def block_offset(degree):
    offset = 0
    for lower in range(degree):
        offset += (2 * min(lower, MMAX) + 1) * (2 * lower + 1)
    return offset


def entry_index(degree, order, column):
    row = min(degree, MMAX) + order
    return block_offset(degree) + row * (2 * degree + 1) + column


def dot(left, right, dims, precision=None):
    return lax.dot_general(
        left, right, (dims, ((), ())), preferred_element_type=F32, precision=precision
    )


NN = ((1,), (0,))
NT = ((1,), (1,))
TN = ((0,), (0,))


def to_rows(values):
    nodes, coef, ch = values.shape
    padded = jnp.pad(values, ((0, 0), (0, QUARTERS * WIDTH - coef), (0, 0)))
    return (
        padded.reshape(nodes, QUARTERS, WIDTH * ch)
        .transpose(1, 0, 2)
        .reshape(QUARTERS * nodes, WIDTH * ch)
    )


def from_rows(rows, nodes, coef, ch):
    whole = rows.reshape(QUARTERS, nodes, WIDTH * ch).transpose(1, 0, 2)
    return whole.reshape(nodes, QUARTERS * WIDTH, ch)[:, :coef]


def gather_kernel(peers, x_ref, out_ref, send_sem, recv_sem):
    me = lax.axis_index("graph")
    rows = x_ref.shape[0]
    barrier = pltpu.get_barrier_semaphore()
    for d in range(1, peers):
        pl.semaphore_signal(
            barrier, inc=1, device_id={"graph": lax.rem(me + d, peers)}, device_id_type=MESH
        )
    pl.semaphore_wait(barrier, peers - 1)
    mine = pl.ds(pl.multiple_of(me * rows, rows), rows)
    copies = []
    for d in range(1, peers):
        copy = pltpu.make_async_remote_copy(
            src_ref=x_ref,
            dst_ref=out_ref.at[mine],
            send_sem=send_sem.at[d - 1],
            recv_sem=recv_sem.at[d - 1],
            device_id={"graph": lax.rem(me + d, peers)},
            device_id_type=MESH,
        )
        copy.start()
        copies.append(copy)
    out_ref[mine] = x_ref[...]
    for copy in copies:
        copy.wait()


def gather_nodes(x, peers):
    return pl.pallas_call(
        functools.partial(gather_kernel, peers),
        name="gather_nodes",
        out_shape=jax.ShapeDtypeStruct((peers * x.shape[0], x.shape[1]), x.dtype),
        in_specs=[pl.BlockSpec(memory_space=pltpu.VMEM)],
        out_specs=pl.BlockSpec(memory_space=pltpu.VMEM),
        scratch_shapes=[
            pltpu.SemaphoreType.DMA((peers - 1,)),
            pltpu.SemaphoreType.DMA((peers - 1,)),
        ],
        compiler_params=pltpu.CompilerParams(
            collective_id=0, has_side_effects=True, vmem_limit_bytes=24 * 2**20
        ),
    )(x)


def shard_plan(peers, ch, heads_padded):
    plan, at = [], 0
    for which, degrees in enumerate((LMAX + 1, LMAX, LMAX, LMAX - 1, LMAX - 1)):
        rows = degrees * ch // peers
        for cb in range(degrees):
            plan.append((which, cb, at, rows))
            at += rows
    rows = (LMAX + 1) * ch // peers
    plan.append((5, 0, at, rows))
    return plan, at + rows


def compute_kernel(
    peers, nodes, slots, heads, plan, packed,
    g_ref, cot_ref, wig_ref, wz_ref, w1r_ref, w1i_ref, w2r_ref, w2i_ref, wa_ref,
    src_ref, dst_ref, req_ref, count_ref,
    *rest,
):
    if packed:
        (t_ref, n_ref), rest = rest[:2], rest[2:]
    else:
        (tz_ref, t1r_ref, t1i_ref, t2r_ref, t2i_ref, ta_ref, n_ref), rest = rest[:7], rest[7:]
    (srcT, cotT, izT, i1T, i2T, iz, i1, i2, bT, oh_s, igT, sgT, gz, g1, g2, bk) = rest
    ch = 128
    edges = src_ref.shape[1]
    per = QUARTERS * nodes
    k = peers * per

    src = src_ref[...]
    base = jnp.zeros((1, edges), jnp.int32)
    for s in range(peers * slots):
        base = jnp.where(src == s, (s // slots) * per + req_ref[s // slots, s % slots], base)
    iota_k = lax.broadcasted_iota(jnp.int32, (k, edges), 0)
    for q in range(QUARTERS):
        hot = jnp.where(iota_k == base + q * nodes, 1.0, 0.0).astype(BF)
        oh_s[q] = hot
        srcT[pl.ds(q * WIDTH * ch, WIDTH * ch), :] = dot(g_ref[...], hot, TN)
    live = lax.broadcasted_iota(jnp.int32, (1, edges), 1) < count_ref[0]
    target = jnp.where(live, dst_ref[...], -per)
    iota_c = lax.broadcasted_iota(jnp.int32, (per, edges), 0)
    for q in range(QUARTERS):
        hot = jnp.where(iota_c == target + q * nodes, 1.0, 0.0).astype(BF)
        cotT[pl.ds(q * WIDTH * ch, WIDTH * ch), :] = dot(cot_ref[...], hot, TN)

    firsts = {0: 0, 1: LMAX + 1, -1: 2 * LMAX + 1, 2: 3 * LMAX + 1, -2: 4 * LMAX}

    def block_of(degree, order):
        return firsts[order] + degree - abs(order)

    def rotate_step(step, carry):
        at = step * CHUNK
        for degree in range(LMAX + 1):
            reach = min(degree, MMAX)
            for source, is_cot in ((srcT, False), (cotT, True)):
                acc = {}
                for column in range(2 * degree + 1):
                    row0 = (degree * degree + column) * ch
                    value = source[pl.ds(pl.multiple_of(row0 + at, CHUNK), CHUNK), :]
                    for order in range(-reach, reach + 1):
                        index = entry_index(degree, order, column)
                        term = wig_ref[index : index + 1, :] * value
                        acc[order] = acc[order] + term if order in acc else term
                for order in range(-reach, reach + 1):
                    if is_cot:
                        row0 = block_of(degree, order) * ch
                        bT[pl.ds(pl.multiple_of(row0 + at, CHUNK), CHUNK), :] = acc[order]
                        continue
                    row0 = (degree - abs(order)) * ch
                    rows = pl.ds(pl.multiple_of(row0 + at, CHUNK), CHUNK)
                    rounded = acc[order].astype(BF)
                    if order == 0:
                        izT[rows, :] = rounded
                    else:
                        half = 0 if order > 0 else edges
                        held = i1T if abs(order) == 1 else i2T
                        held[rows, half : half + edges] = rounded
        return carry

    lax.fori_loop(0, ch // CHUNK, rotate_step, 0)

    def turn(block):
        return jnp.transpose(block)

    for j in range(LMAX + 1):
        cols = slice(j * ch, (j + 1) * ch)
        iz[:, cols] = turn(izT[cols, :].astype(F32)).astype(BF)
    for j in range(LMAX):
        cols = slice(j * ch, (j + 1) * ch)
        for half in range(2):
            lanes = slice(half * edges, (half + 1) * edges)
            i1[lanes, cols] = turn(i1T[cols, lanes].astype(F32)).astype(BF)
            if j < LMAX - 1:
                i2[lanes, cols] = turn(i2T[cols, lanes].astype(F32)).astype(BF)
    blocks = 5 * LMAX - 1
    for j in range(blocks):
        bk[j] = turn(bT[j * ch : (j + 1) * ch, :])

    out_zero = dot(iz[...], wz_ref[...], NN)
    zero_rounded = out_zero.astype(BF)
    agreement = jnp.zeros((edges, ch), F32)
    for j in range(LMAX + 1):
        agreement = agreement + bk[j] * out_zero[:, j * ch : (j + 1) * ch]
    for order, degrees, held, re_ref, im_ref in (
        (1, LMAX, i1, w1r_ref, w1i_ref),
        (2, LMAX - 1, i2, w2r_ref, w2i_ref),
    ):
        with_re = dot(held[...], re_ref[...], NN)
        with_im = dot(held[...], im_ref[...], NN)
        out_p = with_re[:edges] - with_im[edges:]
        out_n = with_im[:edges] + with_re[edges:]
        for j in range(degrees):
            cols = slice(j * ch, (j + 1) * ch)
            agreement = agreement + bk[firsts[order] + j] * out_p[:, cols]
            agreement = agreement + bk[firsts[-order] + j] * out_n[:, cols]

    wa = wa_ref[...]
    weighting = jax.nn.sigmoid(dot(zero_rounded, wa, NN))
    head_of = lax.broadcasted_iota(jnp.int32, (ch, ch), 0) // (ch // heads)
    member = jnp.where(head_of == lax.broadcasted_iota(jnp.int32, (ch, ch), 1), 1.0, 0.0)
    exact = lax.Precision.HIGHEST
    head_sum = dot(agreement, member, NN, exact)
    logit_grad = (head_sum * weighting * (1.0 - weighting)).astype(BF)
    spread = dot(weighting, member, NT, exact)

    from_logit = dot(logit_grad, wa, NT)
    for j in range(LMAX + 1):
        cols = slice(j * ch, (j + 1) * ch)
        gz[:, cols] = (bk[j] * spread + from_logit[:, cols]).astype(BF)
    for order, degrees, held in ((1, LMAX, g1), (2, LMAX - 1, g2)):
        for j in range(degrees):
            cols = slice(j * ch, (j + 1) * ch)
            plus = (bk[firsts[order] + j] * spread).astype(BF)
            minus = (bk[firsts[-order] + j] * spread).astype(BF)
            held[0:edges, cols] = plus
            held[edges : 2 * edges, cols] = minus
            held[2 * edges : 3 * edges, cols] = -plus

    terms = (
        (0, lambda: dot(izT[...], gz[...], NN)),
        (1, lambda: dot(i1T[...], g1[0 : 2 * edges, :], NN)),
        (2, lambda: dot(i1T[...], g1[edges : 3 * edges, :], NN)),
        (3, lambda: dot(i2T[...], g2[0 : 2 * edges, :], NN)),
        (4, lambda: dot(i2T[...], g2[edges : 3 * edges, :], NN)),
        (5, lambda: dot(zero_rounded, logit_grad, TN)),
    )
    for which, make in terms:
        value = make().astype(BF)
        if not packed:
            (tz_ref, t1r_ref, t1i_ref, t2r_ref, t2i_ref, ta_ref)[which][...] = value
            continue
        for owner, cb, at, rows in plan:
            if owner != which:
                continue
            for g in range(peers):
                t_ref[g, at : at + rows, :] = value[
                    g * rows : (g + 1) * rows, cb * ch : (cb + 1) * ch
                ]
    if packed:
        used = plan[-1][2] + plan[-1][3]
        spare = t_ref.shape[1] - used
        if spare:
            for g in range(peers):
                t_ref[g, used : used + spare, :] = jnp.zeros((spare, ch), BF)

    def put(block, degrees, value):
        igT[block * ch : (block + degrees) * ch, :] = value

    put(0, LMAX + 1, dot(wz_ref[...], gz[...], NT))
    for order, degrees, held, re_ref, im_ref in (
        (1, LMAX, g1, w1r_ref, w1i_ref),
        (2, LMAX - 1, g2, w2r_ref, w2i_ref),
    ):
        both = held[0 : 2 * edges, :]
        with_re = dot(re_ref[...], both, NT)
        with_im = dot(im_ref[...], both, NT)
        put(firsts[order], degrees, with_re[:, :edges] + with_im[:, edges:])
        put(firsts[-order], degrees, with_re[:, edges:] - with_im[:, :edges])

    def unrotate_step(step, carry):
        at = step * CHUNK
        for degree in range(LMAX + 1):
            reach = min(degree, MMAX)
            held = {}
            for order in range(-reach, reach + 1):
                row0 = block_of(degree, order) * ch
                held[order] = igT[pl.ds(pl.multiple_of(row0 + at, CHUNK), CHUNK), :]
            for column in range(2 * degree + 1):
                total = None
                for order in range(-reach, reach + 1):
                    index = entry_index(degree, order, column)
                    term = wig_ref[index : index + 1, :] * held[order]
                    total = term if total is None else total + term
                row0 = (degree * degree + column) * ch
                sgT[pl.ds(pl.multiple_of(row0 + at, CHUNK), CHUNK), :] = total.astype(BF)
        return carry

    lax.fori_loop(0, ch // CHUNK, unrotate_step, 0)
    tail = QUARTERS * WIDTH - NCOEF
    if tail:
        sgT[NCOEF * ch : (NCOEF + tail) * ch, :] = jnp.zeros((tail * ch, edges), BF)
    total = None
    for q in range(QUARTERS):
        part = dot(oh_s[q], sgT[q * WIDTH * ch : (q + 1) * WIDTH * ch, :], NT)
        total = part if total is None else total + part
    n_ref[...] = total.astype(BF)


def compute(peers, nodes, slots, heads, plan, rows_padded, packed, *args):
    ch = 128
    edges = args[9].shape[1]
    wide, mid, low = (LMAX + 1) * ch, LMAX * ch, (LMAX - 1) * ch
    blocks = 5 * LMAX - 1
    k = peers * QUARTERS * nodes
    if packed:
        outs = [jax.ShapeDtypeStruct((peers, rows_padded, ch), BF)]
    else:
        outs = [
            jax.ShapeDtypeStruct(shape, BF)
            for shape in ((wide, wide), (mid, mid), (mid, mid), (low, low), (low, low), (wide, ch))
        ]
    outs.append(jax.ShapeDtypeStruct((k, WIDTH * ch), BF))
    vmem = pl.BlockSpec(memory_space=pltpu.VMEM)
    smem = pl.BlockSpec(memory_space=pltpu.SMEM)
    coefs = QUARTERS * WIDTH * ch
    return pl.pallas_call(
        functools.partial(compute_kernel, peers, nodes, slots, heads, plan, packed),
        name="edge_backward",
        out_shape=outs,
        in_specs=[vmem] * 11 + [smem] * 2,
        out_specs=[vmem] * len(outs),
        scratch_shapes=[
            pltpu.VMEM((coefs, edges), F32),
            pltpu.VMEM((coefs, edges), F32),
            pltpu.VMEM((wide, edges), BF),
            pltpu.VMEM((mid, 2 * edges), BF),
            pltpu.VMEM((low, 2 * edges), BF),
            pltpu.VMEM((edges, wide), BF),
            pltpu.VMEM((2 * edges, mid), BF),
            pltpu.VMEM((2 * edges, low), BF),
            pltpu.VMEM((blocks * ch, edges), F32),
            pltpu.VMEM((QUARTERS, k, edges), BF),
            pltpu.VMEM((blocks * ch, edges), F32),
            pltpu.VMEM((coefs, edges), BF),
            pltpu.VMEM((edges, wide), BF),
            pltpu.VMEM((3 * edges, mid), BF),
            pltpu.VMEM((3 * edges, low), BF),
            pltpu.VMEM((blocks, edges, ch), F32),
        ],
        compiler_params=pltpu.CompilerParams(vmem_limit_bytes=56 * 2**20),
    )(*args)


def reduce_kernel(
    ny, nx, nz, h,
    t_ref, n_ref, out_ref, node_ref,
    r0, r1y, r1x, r2x, r2y, r3, mine, gathered, nodes_in, send_sem, recv_sem,
):
    dp = lax.axis_index("dp")
    gi = lax.axis_index("graph")
    core, y = lax.rem(dp, 2), dp // 2
    x, z = lax.rem(gi, nx), gi // nx
    peers = nx * nz
    ndp = 2 * ny
    chn = 128

    def at_y(v):
        return {"dp": v * 2 + core}

    def at_x(v):
        return {"graph": z * nx + v}

    def at_z(v):
        return {"graph": v * nx + x}

    barrier = pltpu.get_barrier_semaphore()
    for d in range(1, ndp):
        pl.semaphore_signal(
            barrier, inc=1, device_id={"dp": lax.rem(dp + d, ndp)}, device_id_type=MESH
        )
    for d in range(1, peers):
        pl.semaphore_signal(
            barrier, inc=1, device_id={"graph": lax.rem(gi + d, peers)}, device_id_type=MESH
        )
    pl.semaphore_wait(barrier, ndp - 1 + peers - 1)

    used = [0]

    def send(source, target, device):
        i = used[0]
        used[0] += 1
        copy = pltpu.make_async_remote_copy(
            src_ref=source, dst_ref=target, send_sem=send_sem.at[i], recv_sem=recv_sem.at[i],
            device_id=device, device_id_type=MESH,
        )
        copy.start()
        return copy

    def span(index, size):
        return pl.ds(pl.multiple_of(index * size, 16), size)

    yh = ny * h
    started = []
    first = []
    for part in range(2):
        first.append(
            send(t_ref.at[:, span(part * 2 + (1 - core), yh)], r0.at[part], {"dp": y * 2 + 1 - core})
        )
    node_copies = []
    rows = node_ref.shape[0]
    for d in range(1, peers):
        to = lax.rem(gi + d, peers)
        node_copies.append(send(n_ref.at[span(to, rows)], nodes_in.at[d - 1], {"graph": to}))

    def add_first(part):
        first[part].wait_recv()
        own = span(part * 2 + core, yh)

        def step(g, carry):
            r0[part, g] = (r0[part, g].astype(F32) + t_ref[g, own].astype(F32)).astype(BF)
            return carry

        lax.fori_loop(0, peers, step, 0)

    add_first(0)
    along_y = []
    for d in range(1, ny):
        to = lax.rem(y + d, ny)
        along_y.append(send(r0.at[0, :, span(to, h)], r1y.at[d - 1], at_y(to)))
    add_first(1)
    along_x = []
    for d in range(1, nx):
        to = lax.rem(x + d, nx)
        along_x.append(
            [send(r0.at[1, zz * nx + to], r1x.at[d - 1, zz], at_x(to)) for zz in range(nz)]
        )

    for copy in along_y:
        copy.wait_recv()

    def sum_y(g, carry):
        total = r0[0, g, span(y, h)].astype(F32)
        for d in range(1, ny):
            total = total + r1y[d - 1, g].astype(F32)
        r1y[ny - 1, g] = total.astype(BF)
        return carry

    lax.fori_loop(0, peers, sum_y, 0)
    second_x = []
    for d in range(1, nx):
        to = lax.rem(x + d, nx)
        second_x.append(
            [send(r1y.at[ny - 1, zz * nx + to], r2x.at[d - 1, zz], at_x(to)) for zz in range(nz)]
        )

    for group in along_x:
        for copy in group:
            copy.wait_recv()

    def sum_x(zz, carry):
        total = r0[1, zz * nx + x].astype(F32)
        for d in range(1, nx):
            total = total + r1x[d - 1, zz].astype(F32)
        r1x[nx - 1, zz] = total.astype(BF)
        return carry

    lax.fori_loop(0, nz, sum_x, 0)
    second_y = []
    for d in range(1, ny):
        to = lax.rem(y + d, ny)
        second_y.append(send(r1x.at[nx - 1, :, span(to, h)], r2y.at[d - 1], at_y(to)))

    for group in second_x:
        for copy in group:
            copy.wait_recv()

    def sum_2x(zz, carry):
        total = r1y[ny - 1, zz * nx + x].astype(F32)
        for d in range(1, nx):
            total = total + r2x[d - 1, zz].astype(F32)
        r2x[nx - 1, zz] = total.astype(BF)
        return carry

    lax.fori_loop(0, nz, sum_2x, 0)
    third = [[], []]
    for d in range(1, nz):
        to = lax.rem(z + d, nz)
        third[0].append(send(r2x.at[nx - 1, to], r3.at[0, d - 1], at_z(to)))
    for copy in second_y:
        copy.wait_recv()

    def sum_2y(zz, carry):
        total = r1x[nx - 1, zz, span(y, h)].astype(F32)
        for d in range(1, ny):
            total = total + r2y[d - 1, zz].astype(F32)
        r2y[ny - 1, zz] = total.astype(BF)
        return carry

    lax.fori_loop(0, nz, sum_2y, 0)
    for d in range(1, nz):
        to = lax.rem(z + d, nz)
        third[1].append(send(r2y.at[ny - 1, to], r3.at[1, d - 1], at_z(to)))

    total = n_ref[span(gi, rows)].astype(F32)
    for d in range(1, peers):
        node_copies[d - 1].wait_recv()
        total = total + nodes_in[d - 1].astype(F32)
    node_ref[...] = total

    last = []
    for part in range(2):
        for copy in third[part]:
            copy.wait_recv()
        total = (r2x[nx - 1, z] if part == 0 else r2y[ny - 1, z]).astype(F32)
        for d in range(1, nz):
            total = total + r3[part, d - 1].astype(F32)
        mine[part] = (total * (1.0 / ndp)).astype(BF)
        for d in range(1, ndp):
            to = lax.rem(dp + d, ndp)
            last.append(send(mine.at[part], gathered.at[part, d - 1], {"dp": to}))
    for part in range(2):
        out_ref[span(part * ndp + core * ny + y, h)] = mine[part]
    for i, copy in enumerate(last):
        part, d = i // (ndp - 1), i % (ndp - 1) + 1
        copy.wait_recv()
        who = lax.rem(dp + ndp - d, ndp)
        out_ref[span(part * ndp + lax.rem(who, 2) * ny + who // 2, h)] = gathered[part, d - 1]
    for copy in first + node_copies + along_y + second_y + third[0] + third[1] + last:
        copy.wait_send()
    for group in along_x + second_x:
        for copy in group:
            copy.wait_send()


def reduce_all(terms, node_terms, ny, nx, nz):
    peers, rows_padded, ch = terms.shape
    ndp = 2 * ny
    h = rows_padded // (2 * ndp)
    rows = node_terms.shape[0] // peers
    sends = 2 + (peers - 1) + 2 * (ny - 1) + 2 * (nx - 1) * nz + 2 * (nz - 1) + 2 * (ndp - 1)
    vmem = pl.BlockSpec(memory_space=pltpu.VMEM)
    return pl.pallas_call(
        functools.partial(reduce_kernel, ny, nx, nz, h),
        name="reduce_all",
        out_shape=[
            jax.ShapeDtypeStruct((rows_padded, ch), BF),
            jax.ShapeDtypeStruct((rows, node_terms.shape[1]), F32),
        ],
        in_specs=[vmem] * 2,
        out_specs=[vmem] * 2,
        scratch_shapes=[
            pltpu.VMEM((2, peers, ny * h, ch), BF),
            pltpu.VMEM((ny, peers, h, ch), BF),
            pltpu.VMEM((nx, nz, ny * h, ch), BF),
            pltpu.VMEM((nx, nz, h, ch), BF),
            pltpu.VMEM((ny, nz, h, ch), BF),
            pltpu.VMEM((2, max(nz - 1, 1), h, ch), BF),
            pltpu.VMEM((2, h, ch), BF),
            pltpu.VMEM((2, ndp - 1, h, ch), BF),
            pltpu.VMEM((peers - 1, rows, node_terms.shape[1]), BF),
            pltpu.SemaphoreType.DMA((sends,)),
            pltpu.SemaphoreType.DMA((sends,)),
        ],
        compiler_params=pltpu.CompilerParams(
            collective_id=1, has_side_effects=True, vmem_limit_bytes=48 * 2**20
        ),
    )(terms, node_terms)


def per_device(
    node_features, cotangent, wigner, w_zero, w_one_re, w_one_im, w_two_re, w_two_im, w_attn,
    src_slot, dst_node, request, edge_count,
):
    peers = lax.axis_size("graph")
    ndp = lax.axis_size("dp")
    ny = ndp // 2
    nx = ny
    nz = peers // nx
    nodes, coef, ch = node_features.shape
    heads = w_attn.shape[1]
    plan, used = shard_plan(peers, ch, ch)
    unit = 16 * 2 * ndp
    rows_padded = -(-used // unit) * unit
    packed = all(rows % 16 == 0 for _, _, _, rows in plan)

    everyone = gather_nodes(to_rows(node_features), peers)
    results = compute(
        peers, nodes, request.shape[2], heads, plan, rows_padded, packed,
        everyone, to_rows(cotangent), wigner, w_zero, w_one_re, w_one_im, w_two_re, w_two_im,
        jnp.pad(w_attn, ((0, 0), (0, ch - heads))),
        src_slot[None, :], dst_node[None, :], request[0], edge_count,
    )
    node_terms = results[-1]
    if packed:
        terms = results[0]
    else:
        pieces = [
            results[which].reshape(peers, rows, -1)[:, :, cb * ch : (cb + 1) * ch]
            for which, cb, _, rows in plan
        ]
        pieces.append(jnp.zeros((peers, rows_padded - used, ch), BF))
        terms = jnp.concatenate(pieces, axis=1)
    shard, node_rows = reduce_all(terms, node_terms, ny, nx, nz)
    node_grad = from_rows(node_rows, nodes, coef, ch)
    outs = []
    for which in range(5):
        mine = [p for p in plan if p[0] == which]
        at, rows = mine[0][2], mine[0][3]
        block = shard[at : at + rows * len(mine)].reshape(len(mine), rows, ch)
        outs.append(block.transpose(1, 0, 2).reshape(rows, -1).astype(F32))
    _, _, at, rows = plan[-1]
    outs.append(shard[at : at + rows, :heads].astype(F32))
    return (node_grad, *outs)


def solution(mesh):
    both = ("dp", "graph")
    in_specs = (
        P(both, None, None), P(both, None, None), P(None, both),
        P(), P(), P(), P(), P(), P(),
        P(both), P(both), P(both, None, None), P(both),
    )
    out_specs = (P(both, None, None),) + (P("graph", None),) * 6
    return jax.shard_map(
        per_device, mesh=mesh, in_specs=in_specs, out_specs=out_specs, check_vma=False
    )
```

profile of v0, /device:TPU:0, one launch (start us, length us, event | category | flops | bytes accessed | tf_op | source)
XLA Modules:
  0.0 103.8 jit_solution(12373461629305908195)
XLA Ops:
  1.3 1.3 %copy.29.req_ref = s32[8,2]{1,0:T(8,128)} copy(s32[8,2]{0,1:T(2,128)} %bitcast.57) | data formatting | bytes 128 | tf_op jit(solution)/shard_map/squeeze | solution.py:593
  2.6 0.8 pad.11
  3.5 0.8 pad.12
  4.3 0.6 reshape.65.cot_ref
  4.9 0.9 copy.28
  5.8 0.7 pad.13.wa_ref
  6.6 12.9 %gather_nodes.1.g_ref = bf16[128,1664]{1,0:T(8,128)(2,1)S(1)} custom-call(bf16[16,1664]{1,0:T(8,128)(2,1)S(1)} %reshape.63.x_ref), custom_call_target="tpu_custom_call" | custom-call | tf_op jit(solution)/shard_map/gather_nodes/pallas_call | solution.py:88
  19.5 0.0 copy-start
  19.5 0.8 copy-done
  20.3 15.6 %edge_backward.1 = (bf16[8,2944,128]{2,1,0:T(8,128)(2,1)}, bf16[128,1664]{1,0:T(8,128)(2,1)}) custom-call(bf16[128,1664]{1,0:T(8,128)(2,1)} %copy-done, bf16[16,1664]{1,0:T(8,128)(2,1)} %reshape.65.cot_ref, f32[235,128]{1,0:T(8,128)} %wig_ref.1, bf16[896,896]{1,0:T(8,128)(2,1)} %wz_ref.1, bf16[768,768]{1,0:T(8,128)(2,1)} %w1r_ref.1, ...), custom_call_target="tpu_custom_call" | custom-call | tf_op jit(solution)/shard_map/edge_backward/pallas_call | solution.py:328
  35.8 0.0 copy-start.1
  35.8 1.0 copy-done.1
  36.8 62.8 %reduce_all.1 = (bf16[2944,128]{1,0:T(8,128)(2,1)S(1)}, f32[16,1664]{1,0:T(8,128)S(1)}) custom-call(bf16[8,2944,128]{2,1,0:T(8,128)(2,1)} %get-tuple-element.11.t_ref, bf16[128,1664]{1,0:T(8,128)(2,1)S(1)} %copy-done.1), custom_call_target="tpu_custom_call" | custom-call | tf_op jit(solution)/shard_map/reduce_all/pallas_call | solution.py:544
  99.6 0.6 slice.28
  100.3 0.7 copy.35
  101.1 0.8 copy_bitcast_fusion.3
  101.9 0.1 copy.31
  102.0 0.1 copy.32
  102.0 0.9 copy_bitcast_fusion.1
  103.0 0.8 copy.46
  (9 shorter events, 0.2 us)
Async XLA Ops:
  19.5 0.8 copy-start
  35.8 1.0 copy-start.1
where the time goes:
time: 105 us; the launch traced here: 104 us
  Pallas kernels  91.2 us (87%)
  local copies, waits for them, and re-layouts  11.2 us (11%)
  between operations  1.39 us (1%)
    pallas_call x1, Pallas kernels, reduce_all(): pl.pallas_call(functools.partial(reduce_kernel, ny, nx, nz, h), name='red...  62.8 us
    pallas_call x1, Pallas kernels, compute(): pl.pallas_call(functools.partial(compute_kernel, peers, nodes, slots, hea...  15.6 us
    pallas_call x1, Pallas kernels, gather_nodes(): pl.pallas_call(functools.partial(gather_kernel, peers), name='gather_node...  12.9 us
    unnamed x7, local copies, waits for them, and re-layouts  4.13 us

commit v1 on v0

--- a/solution.py
+++ b/solution.py
@@ -17,6 +17,7 @@
 QUARTERS = 4
 WIDTH = -(-NCOEF // QUARTERS)
 CHUNK = 32
+PARTS = 4
 
 
 def block_offset(degree):
@@ -57,43 +58,58 @@
     return whole.reshape(nodes, QUARTERS * WIDTH, ch)[:, :coef]
 
 
-def gather_kernel(peers, x_ref, out_ref, send_sem, recv_sem):
+def gather_kernel(nx, nz, x_ref, out_ref, send_sem, recv_sem):
     me = lax.axis_index("graph")
+    x, z = lax.rem(me, nx), me // nx
     rows = x_ref.shape[0]
+    along_x = [z * nx + lax.rem(x + d, nx) for d in range(1, nx)]
+    along_z = [lax.rem(z + d, nz) * nx + x for d in range(1, nz)]
     barrier = pltpu.get_barrier_semaphore()
-    for d in range(1, peers):
-        pl.semaphore_signal(
-            barrier, inc=1, device_id={"graph": lax.rem(me + d, peers)}, device_id_type=MESH
-        )
-    pl.semaphore_wait(barrier, peers - 1)
-    mine = pl.ds(pl.multiple_of(me * rows, rows), rows)
+    for to in along_x + along_z:
+        pl.semaphore_signal(barrier, inc=1, device_id={"graph": to}, device_id_type=MESH)
+    pl.semaphore_wait(barrier, nx - 1 + nz - 1)
+
+    def block(index):
+        return out_ref.at[pl.ds(pl.multiple_of(index * rows, rows), rows)]
+
     copies = []
-    for d in range(1, peers):
+
+    def send(source, index, to):
+        i = len(copies)
         copy = pltpu.make_async_remote_copy(
-            src_ref=x_ref,
-            dst_ref=out_ref.at[mine],
-            send_sem=send_sem.at[d - 1],
-            recv_sem=recv_sem.at[d - 1],
-            device_id={"graph": lax.rem(me + d, peers)},
-            device_id_type=MESH,
+            src_ref=source, dst_ref=block(index), send_sem=send_sem.at[i],
+            recv_sem=recv_sem.at[i], device_id={"graph": to}, device_id_type=MESH,
         )
         copy.start()
         copies.append(copy)
-    out_ref[mine] = x_ref[...]
-    for copy in copies:
-        copy.wait()
-
-
-def gather_nodes(x, peers):
+        return copy
+
+    over_z = [send(x_ref, me, to) for to in along_z]
+    for to in along_x:
+        send(x_ref, me, to)
+    out_ref[pl.ds(pl.multiple_of(me * rows, rows), rows)] = x_ref[...]
+    for d in range(1, nz):
+        over_z[d - 1].wait_recv()
+        came = lax.rem(z + nz - d, nz) * nx + x
+        for to in along_x:
+            send(block(came), came, to)
+    for i, copy in enumerate(copies):
+        copy.wait_send()
+        if i >= nz - 1:
+            copy.wait_recv()
+
+
+def gather_nodes(x, nx, nz):
+    sends = nz - 1 + (nx - 1) * nz
     return pl.pallas_call(
-        functools.partial(gather_kernel, peers),
+        functools.partial(gather_kernel, nx, nz),
         name="gather_nodes",
-        out_shape=jax.ShapeDtypeStruct((peers * x.shape[0], x.shape[1]), x.dtype),
+        out_shape=jax.ShapeDtypeStruct((nx * nz * x.shape[0], x.shape[1]), x.dtype),
         in_specs=[pl.BlockSpec(memory_space=pltpu.VMEM)],
         out_specs=pl.BlockSpec(memory_space=pltpu.VMEM),
         scratch_shapes=[
-            pltpu.SemaphoreType.DMA((peers - 1,)),
-            pltpu.SemaphoreType.DMA((peers - 1,)),
+            pltpu.SemaphoreType.DMA((sends,)),
+            pltpu.SemaphoreType.DMA((sends,)),
         ],
         compiler_params=pltpu.CompilerParams(
             collective_id=0, has_side_effects=True, vmem_limit_bytes=24 * 2**20
@@ -108,7 +124,7 @@
         for cb in range(degrees):
             plan.append((which, cb, at, rows))
             at += rows
-    rows = (LMAX + 1) * ch // peers
+    rows = (LMAX + 1) * ch // peers // 2
     plan.append((5, 0, at, rows))
     return plan, at + rows
 
@@ -247,7 +263,21 @@
         (5, lambda: dot(zero_rounded, logit_grad, TN)),
     )
     for which, make in terms:
-        value = make().astype(BF)
+        value = make()
+        if which == 5:
+            value = value.reshape(peers, 2, -1, ch)
+            value = value[:, 0] + pltpu.roll(value[:, 1].reshape(-1, ch), heads, 1).reshape(
+                peers, -1, ch
+            )
+            if packed:
+                at, rows = plan[-1][2:]
+                spare = t_ref.shape[1] - at - rows
+                if spare:
+                    value = jnp.concatenate([value, jnp.zeros((peers, spare, ch), F32)], 1)
+                t_ref[:, at:, :] = value.astype(BF)
+                continue
+            value = value.reshape(-1, ch)
+        value = value.astype(BF)
         if not packed:
             (tz_ref, t1r_ref, t1i_ref, t2r_ref, t2i_ref, ta_ref)[which][...] = value
             continue
@@ -258,13 +288,6 @@
                 t_ref[g, at : at + rows, :] = value[
                     g * rows : (g + 1) * rows, cb * ch : (cb + 1) * ch
                 ]
-    if packed:
-        used = plan[-1][2] + plan[-1][3]
-        spare = t_ref.shape[1] - used
-        if spare:
-            for g in range(peers):
-                t_ref[g, used : used + spare, :] = jnp.zeros((spare, ch), BF)
-
     def put(block, degrees, value):
         igT[block * ch : (block + degrees) * ch, :] = value
 
@@ -319,7 +342,7 @@
     else:
         outs = [
             jax.ShapeDtypeStruct(shape, BF)
-            for shape in ((wide, wide), (mid, mid), (mid, mid), (low, low), (low, low), (wide, ch))
+            for shape in ((wide, wide), (mid, mid), (mid, mid), (low, low), (low, low), (wide // 2, ch))
         ]
     outs.append(jax.ShapeDtypeStruct((k, WIDTH * ch), BF))
     vmem = pl.BlockSpec(memory_space=pltpu.VMEM)
@@ -356,7 +379,7 @@
 def reduce_kernel(
     ny, nx, nz, h,
     t_ref, n_ref, out_ref, node_ref,
-    r0, r1y, r1x, r2x, r2y, r3, mine, gathered, nodes_in, send_sem, recv_sem,
+    own, r0, r1y, r1x, r2x, r2y, r3, nodes_in, send_sem, recv_sem, own_sem,
 ):
     dp = lax.axis_index("dp")
     gi = lax.axis_index("graph")
@@ -364,7 +387,7 @@
     x, z = lax.rem(gi, nx), gi // nx
     peers = nx * nz
     ndp = 2 * ny
-    chn = 128
+    yh = ny * h
 
     def at_y(v):
         return {"dp": v * 2 + core}
@@ -374,6 +397,19 @@
 
     def at_z(v):
         return {"graph": v * nx + x}
+
+    other_core = {"dp": y * 2 + 1 - core}
+
+    def span(index, size):
+        return pl.ds(pl.multiple_of(index * size, 16), size)
+
+    locals_ = []
+    for part in range(PARTS):
+        copy = pltpu.make_async_copy(
+            t_ref.at[:, :, span(part * 2 + core, yh)], own.at[part], own_sem.at[part]
+        )
+        copy.start()
+        locals_.append(copy)
 
     barrier = pltpu.get_barrier_semaphore()
     for d in range(1, ndp):
@@ -386,122 +422,112 @@
         )
     pl.semaphore_wait(barrier, ndp - 1 + peers - 1)
 
-    used = [0]
+    sent = []
 
     def send(source, target, device):
-        i = used[0]
-        used[0] += 1
+        i = len(sent)
         copy = pltpu.make_async_remote_copy(
             src_ref=source, dst_ref=target, send_sem=send_sem.at[i], recv_sem=recv_sem.at[i],
             device_id=device, device_id_type=MESH,
         )
         copy.start()
+        sent.append(copy)
         return copy
 
-    def span(index, size):
-        return pl.ds(pl.multiple_of(index * size, 16), size)
-
-    yh = ny * h
-    started = []
+    def arrive(copies):
+        for copy in copies:
+            copy.wait_recv()
+
+    def offsets(me, n):
+        return [(d - 1, lax.rem(me + d, n)) for d in range(1, n)]
+
+    def sum_over_z(target, sources):
+        def step(zz, carry):
+            total = None
+            for source in sources:
+                value = source(zz).astype(F32)
+                total = value if total is None else total + value
+            target[zz] = total.astype(BF)
+            return carry
+
+        lax.fori_loop(0, nz, step, 0)
+
+    parts = range(PARTS)
+    zero = [
+        send(t_ref.at[:, :, span(part * 2 + (1 - core), yh)], r0.at[part], other_core)
+        for part in parts
+    ]
+    rows = node_ref.shape[0]
+    node_copies = []
+    for slot, to in offsets(gi, peers):
+        node_copies.append(send(n_ref.at[span(to, rows)], nodes_in.at[slot], {"graph": to}))
+
     first = []
-    for part in range(2):
-        first.append(
-            send(t_ref.at[:, span(part * 2 + (1 - core), yh)], r0.at[part], {"dp": y * 2 + 1 - core})
-        )
-    node_copies = []
-    rows = node_ref.shape[0]
-    for d in range(1, peers):
-        to = lax.rem(gi + d, peers)
-        node_copies.append(send(n_ref.at[span(to, rows)], nodes_in.at[d - 1], {"graph": to}))
-
-    def add_first(part):
-        first[part].wait_recv()
-        own = span(part * 2 + core, yh)
-
-        def step(g, carry):
-            r0[part, g] = (r0[part, g].astype(F32) + t_ref[g, own].astype(F32)).astype(BF)
-            return carry
-
-        lax.fori_loop(0, peers, step, 0)
-
-    add_first(0)
-    along_y = []
-    for d in range(1, ny):
-        to = lax.rem(y + d, ny)
-        along_y.append(send(r0.at[0, :, span(to, h)], r1y.at[d - 1], at_y(to)))
-    add_first(1)
-    along_x = []
-    for d in range(1, nx):
-        to = lax.rem(x + d, nx)
-        along_x.append(
-            [send(r0.at[1, zz * nx + to], r1x.at[d - 1, zz], at_x(to)) for zz in range(nz)]
-        )
-
-    for copy in along_y:
-        copy.wait_recv()
-
-    def sum_y(g, carry):
-        total = r0[0, g, span(y, h)].astype(F32)
-        for d in range(1, ny):
-            total = total + r1y[d - 1, g].astype(F32)
-        r1y[ny - 1, g] = total.astype(BF)
-        return carry
-
-    lax.fori_loop(0, peers, sum_y, 0)
-    second_x = []
-    for d in range(1, nx):
-        to = lax.rem(x + d, nx)
-        second_x.append(
-            [send(r1y.at[ny - 1, zz * nx + to], r2x.at[d - 1, zz], at_x(to)) for zz in range(nz)]
-        )
-
-    for group in along_x:
-        for copy in group:
-            copy.wait_recv()
-
-    def sum_x(zz, carry):
-        total = r0[1, zz * nx + x].astype(F32)
-        for d in range(1, nx):
-            total = total + r1x[d - 1, zz].astype(F32)
-        r1x[nx - 1, zz] = total.astype(BF)
-        return carry
-
-    lax.fori_loop(0, nz, sum_x, 0)
-    second_y = []
-    for d in range(1, ny):
-        to = lax.rem(y + d, ny)
-        second_y.append(send(r1x.at[nx - 1, :, span(to, h)], r2y.at[d - 1], at_y(to)))
-
-    for group in second_x:
-        for copy in group:
-            copy.wait_recv()
-
-    def sum_2x(zz, carry):
-        total = r1y[ny - 1, zz * nx + x].astype(F32)
-        for d in range(1, nx):
-            total = total + r2x[d - 1, zz].astype(F32)
-        r2x[nx - 1, zz] = total.astype(BF)
-        return carry
-
-    lax.fori_loop(0, nz, sum_2x, 0)
-    third = [[], []]
-    for d in range(1, nz):
-        to = lax.rem(z + d, nz)
-        third[0].append(send(r2x.at[nx - 1, to], r3.at[0, d - 1], at_z(to)))
-    for copy in second_y:
-        copy.wait_recv()
-
-    def sum_2y(zz, carry):
-        total = r1x[nx - 1, zz, span(y, h)].astype(F32)
-        for d in range(1, ny):
-            total = total + r2y[d - 1, zz].astype(F32)
-        r2y[ny - 1, zz] = total.astype(BF)
-        return carry
-
-    lax.fori_loop(0, nz, sum_2y, 0)
-    for d in range(1, nz):
-        to = lax.rem(z + d, nz)
-        third[1].append(send(r2y.at[ny - 1, to], r3.at[1, d - 1], at_z(to)))
+    for part in parts:
+        i = part // 2
+        locals_[part].wait()
+        zero[part].wait_recv()
+        sum_over_z(
+            r0.at[part],
+            [lambda zz, part=part: own[part, zz], lambda zz, part=part: r0[part, zz]],
+        )
+        if part % 2 == 0:
+            first.append(
+                [send(r0.at[part, :, :, span(to, h)], r1y.at[i, slot], at_y(to))
+                 for slot, to in offsets(y, ny)]
+            )
+        else:
+            first.append(
+                [send(r0.at[part, :, to], r1x.at[i, slot], at_x(to))
+                 for slot, to in offsets(x, nx)]
+            )
+
+    second = []
+    for part in parts:
+        i = part // 2
+        arrive(first[part])
+        if part % 2 == 0:
+            sum_over_z(
+                r1y.at[i, ny - 1],
+                [lambda zz, part=part: r0[part, zz, :, span(y, h)]]
+                + [lambda zz, i=i, d=d: r1y[i, d, zz] for d in range(ny - 1)],
+            )
+            second.append(
+                [send(r1y.at[i, ny - 1, :, to], r2x.at[i, slot], at_x(to))
+                 for slot, to in offsets(x, nx)]
+            )
+        else:
+            sum_over_z(
+                r1x.at[i, nx - 1],
+                [lambda zz, part=part: r0[part, zz, x]]
+                + [lambda zz, i=i, d=d: r1x[i, d, zz] for d in range(nx - 1)],
+            )
+            second.append(
+                [send(r1x.at[i, nx - 1, :, span(to, h)], r2y.at[i, slot], at_y(to))
+                 for slot, to in offsets(y, ny)]
+            )
+
+    third = []
+    for part in parts:
+        i = part // 2
+        arrive(second[part])
+        if part % 2 == 0:
+            held = r2x.at[i, nx - 1]
+            sum_over_z(
+                held,
+                [lambda zz, i=i: r1y[i, ny - 1, zz, x]]
+                + [lambda zz, i=i, d=d: r2x[i, d, zz] for d in range(nx - 1)],
+            )
+        else:
+            held = r2y.at[i, ny - 1]
+            sum_over_z(
+                held,
+                [lambda zz, i=i: r1x[i, nx - 1, zz, span(y, h)]]
+                + [lambda zz, i=i, d=d: r2y[i, d, zz] for d in range(ny - 1)],
+            )
+        third.append(
+            [send(held.at[to], r3.at[part, slot], at_z(to)) for slot, to in offsets(z, nz)]
+        )
 
     total = n_ref[span(gi, rows)].astype(F32)
     for d in range(1, peers):
@@ -509,37 +535,34 @@
         total = total + nodes_in[d - 1].astype(F32)
     node_ref[...] = total
 
-    last = []
-    for part in range(2):
-        for copy in third[part]:
-            copy.wait_recv()
-        total = (r2x[nx - 1, z] if part == 0 else r2y[ny - 1, z]).astype(F32)
-        for d in range(1, nz):
-            total = total + r3[part, d - 1].astype(F32)
-        mine[part] = (total * (1.0 / ndp)).astype(BF)
-        for d in range(1, ndp):
-            to = lax.rem(dp + d, ndp)
-            last.append(send(mine.at[part], gathered.at[part, d - 1], {"dp": to}))
-    for part in range(2):
-        out_ref[span(part * ndp + core * ny + y, h)] = mine[part]
-    for i, copy in enumerate(last):
-        part, d = i // (ndp - 1), i % (ndp - 1) + 1
-        copy.wait_recv()
-        who = lax.rem(dp + ndp - d, ndp)
-        out_ref[span(part * ndp + lax.rem(who, 2) * ny + who // 2, h)] = gathered[part, d - 1]
-    for copy in first + node_copies + along_y + second_y + third[0] + third[1] + last:
+    fourth = []
+    for part in parts:
+        i = part // 2
+        arrive(third[part])
+        total = (r2x[i, nx - 1, z] if part % 2 == 0 else r2y[i, ny - 1, z]).astype(F32)
+        for d in range(nz - 1):
+            total = total + r3[part, d].astype(F32)
+        mine = span((part * 2 + core) * ny + y, h)
+        out_ref[mine] = (total * (1.0 / ndp)).astype(BF)
+        fourth.append(
+            [send(out_ref.at[mine], out_ref.at[mine], at_y(to)) for _, to in offsets(y, ny)]
+        )
+    fifth = []
+    for part in parts:
+        arrive(fourth[part])
+        half = span(part * 2 + core, yh)
+        fifth.append(send(out_ref.at[half], out_ref.at[half], other_core))
+    arrive(fifth)
+    for copy in sent:
         copy.wait_send()
-    for group in along_x + second_x:
-        for copy in group:
-            copy.wait_send()
 
 
 def reduce_all(terms, node_terms, ny, nx, nz):
     peers, rows_padded, ch = terms.shape
     ndp = 2 * ny
-    h = rows_padded // (2 * ndp)
+    h = rows_padded // (PARTS * ndp)
     rows = node_terms.shape[0] // peers
-    sends = 2 + (peers - 1) + 2 * (ny - 1) + 2 * (nx - 1) * nz + 2 * (nz - 1) + 2 * (ndp - 1)
+    sends = 2 * PARTS + (peers - 1) + PARTS * (2 * (ny - 1) + nx - 1 + nz - 1)
     vmem = pl.BlockSpec(memory_space=pltpu.VMEM)
     return pl.pallas_call(
         functools.partial(reduce_kernel, ny, nx, nz, h),
@@ -548,25 +571,25 @@
             jax.ShapeDtypeStruct((rows_padded, ch), BF),
             jax.ShapeDtypeStruct((rows, node_terms.shape[1]), F32),
         ],
-        in_specs=[vmem] * 2,
+        in_specs=[pl.BlockSpec(memory_space=pl.ANY), vmem],
         out_specs=[vmem] * 2,
         scratch_shapes=[
-            pltpu.VMEM((2, peers, ny * h, ch), BF),
-            pltpu.VMEM((ny, peers, h, ch), BF),
-            pltpu.VMEM((nx, nz, ny * h, ch), BF),
-            pltpu.VMEM((nx, nz, h, ch), BF),
-            pltpu.VMEM((ny, nz, h, ch), BF),
-            pltpu.VMEM((2, max(nz - 1, 1), h, ch), BF),
-            pltpu.VMEM((2, h, ch), BF),
-            pltpu.VMEM((2, ndp - 1, h, ch), BF),
+            pltpu.VMEM((PARTS, nz, nx, ny * h, ch), BF),
+            pltpu.VMEM((PARTS, nz, nx, ny * h, ch), BF),
+            pltpu.VMEM((PARTS // 2, ny, nz, nx, h, ch), BF),
+            pltpu.VMEM((PARTS // 2, nx, nz, ny * h, ch), BF),
+            pltpu.VMEM((PARTS // 2, nx, nz, h, ch), BF),
+            pltpu.VMEM((PARTS // 2, ny, nz, h, ch), BF),
+            pltpu.VMEM((PARTS, max(nz - 1, 1), h, ch), BF),
             pltpu.VMEM((peers - 1, rows, node_terms.shape[1]), BF),
             pltpu.SemaphoreType.DMA((sends,)),
             pltpu.SemaphoreType.DMA((sends,)),
+            pltpu.SemaphoreType.DMA((PARTS,)),
         ],
         compiler_params=pltpu.CompilerParams(
-            collective_id=1, has_side_effects=True, vmem_limit_bytes=48 * 2**20
+            collective_id=1, has_side_effects=True, vmem_limit_bytes=56 * 2**20
         ),
-    )(terms, node_terms)
+    )(terms.reshape(nz, nx, rows_padded, ch), node_terms)
 
 
 def per_device(
@@ -581,11 +604,12 @@
     nodes, coef, ch = node_features.shape
     heads = w_attn.shape[1]
     plan, used = shard_plan(peers, ch, ch)
-    unit = 16 * 2 * ndp
+    unit = 16 * PARTS * ndp
     rows_padded = -(-used // unit) * unit
-    packed = all(rows % 16 == 0 for _, _, _, rows in plan)
-
-    everyone = gather_nodes(to_rows(node_features), peers)
+    packed = all(rows % 16 == 0 for which, _, _, rows in plan if which < 5)
+    packed = packed and plan[-1][3] % 8 == 0
+
+    everyone = gather_nodes(to_rows(node_features), nx, nz)
     results = compute(
         peers, nodes, request.shape[2], heads, plan, rows_padded, packed,
         everyone, to_rows(cotangent), wigner, w_zero, w_one_re, w_one_im, w_two_re, w_two_im,
@@ -611,7 +635,9 @@
         block = shard[at : at + rows * len(mine)].reshape(len(mine), rows, ch)
         outs.append(block.transpose(1, 0, 2).reshape(rows, -1).astype(F32))
     _, _, at, rows = plan[-1]
-    outs.append(shard[at : at + rows, :heads].astype(F32))
+    folded = shard[at : at + rows, : 2 * heads]
+    folded = jnp.concatenate([folded[:, :heads], folded[:, heads:]], 0)
+    outs.append(folded.astype(F32))
     return (node_grad, *outs)
 
 

time: 105 us -> 99.3 us (0.946)
  Pallas kernels: 91.2 us -> 82.4 us
  local copies, waits for them, and re-layouts: 11.2 us -> 14.3 us
    pallas_call x1, Pallas kernels: 62.8 us -> 52.6 us  [reduce_all(): pl.pallas_call(functools.partial(reduce_kernel, ny, nx, nz, h), name='red...]
    slice x3, local copies, waits for them, and re-layouts: 0.05 us -> 2.91 us  [per_device(): block = shard[at:at + rows * len(mine)].reshape(len(mine), rows, ch)]
    unnamed x7 -> x4, local copies, waits for them, and re-layouts: 4.13 us -> 2.46 us
    pallas_call x1, Pallas kernels: 12.9 us -> 14.3 us  [gather_nodes(): pl.pallas_call(functools.partial(gather_kernel, nx, nz), name='gather_nod...]
where the time goes in v1:
time: 99.3 us; the launch traced here: 98.8 us
  Pallas kernels  82.4 us (83%)
  local copies, waits for them, and re-layouts  14.3 us (14%)
  between operations  1.37 us (1%)
    pallas_call x1, Pallas kernels, reduce_all(): pl.pallas_call(functools.partial(reduce_kernel, ny, nx, nz, h), name='red...  52.6 us
    pallas_call x1, Pallas kernels, compute(): pl.pallas_call(functools.partial(compute_kernel, peers, nodes, slots, hea...  15.5 us
    pallas_call x1, Pallas kernels, gather_nodes(): pl.pallas_call(functools.partial(gather_kernel, nx, nz), name='gather_nod...  14.3 us
    slice x3, local copies, waits for them, and re-layouts, per_device(): block = shard[at:at + rows * len(mine)].reshape(len(mine), rows, ch)  2.91 us
    unnamed x4, local copies, waits for them, and re-layouts  2.46 us

profile of v1, /device:TPU:0, one launch (start us, length us, event | category | flops | bytes accessed | tf_op | source)
XLA Modules:
  0.0 98.8 jit_solution(5728569890778635086)
XLA Ops:
  1.3 1.3 %copy.37.req_ref = s32[8,2]{1,0:T(8,128)} copy(s32[8,2]{0,1:T(2,128)} %bitcast.59) | data formatting | bytes 128 | tf_op jit(solution)/shard_map/squeeze | solution.py:617
  2.6 0.8 pad.11
  3.5 0.8 pad.12
  4.3 0.6 reshape.68.cot_ref
  4.9 0.9 copy.36
  5.8 0.7 pad.13.wa_ref
  6.6 14.3 %gather_nodes.1.g_ref = bf16[128,1664]{1,0:T(8,128)(2,1)S(1)} custom-call(bf16[16,1664]{1,0:T(8,128)(2,1)S(1)} %reshape.66.x_ref), custom_call_target="tpu_custom_call" | custom-call | tf_op jit(solution)/shard_map/gather_nodes/pallas_call | solution.py:104
  20.9 0.0 copy-start
  20.9 0.8 copy-done
  21.7 15.5 %edge_backward.1 = (bf16[8,2816,128]{2,1,0:T(8,128)(2,1)}, bf16[128,1664]{1,0:T(8,128)(2,1)}) custom-call(bf16[128,1664]{1,0:T(8,128)(2,1)} %copy-done, bf16[16,1664]{1,0:T(8,128)(2,1)} %reshape.68.cot_ref, f32[235,128]{1,0:T(8,128)} %wig_ref.1, bf16[896,896]{1,0:T(8,128)(2,1)} %wz_ref.1, bf16[768,768]{1,0:T(8,128)(2,1)} %w1r_ref.1, ...), custom_call_target="tpu_custom_call" | custom-call | tf_op jit(solution)/shard_map/edge_backward/pallas_call | solution.py:351
  37.2 52.6 %reduce_all.1 = (bf16[2816,128]{1,0:T(8,128)(2,1)}, f32[16,1664]{1,0:T(8,128)}) custom-call(bf16[4,2,2816,128]{3,2,1,0:T(8,128)(2,1)} %bitcast.44, bf16[128,1664]{1,0:T(8,128)(2,1)} %get-tuple-element.12.n_ref), custom_call_target="tpu_custom_call" | custom-call | tf_op jit(solution)/shard_map/reduce_all/pallas_call | solution.py:567
  89.7 0.9 reshape.70
  90.7 0.6 slice.35
  91.3 0.9 fusion
  92.2 0.1 copy.43
  92.3 0.1 copy.44
  92.3 0.7 maximum_convert_fusion
  93.0 0.9 slice.28
  94.0 1.0 fusion.1
  94.9 1.0 %fusion.2 = (bf16[576,128]{1,0:T(8,128)(2,1)S(1)}, bf16[576,128]{1,0:T(8,128)(2,1)S(1)}) fusion(bf16[2816,128]{1,0:T(8,128)(2,1)} %get-tuple-element.14), kind=kLoop, calls=%fused_computation.8 | loop fusion | bytes 589824 | tf_op jit(solution)/shard_map/slice | solution.py:635
  96.0 0.8 copy_bitcast_fusion.3
  96.8 0.1 copy.39
  96.9 0.1 copy.40
  97.0 0.9 copy_bitcast_fusion.1
  97.9 0.8 copy.55
  (4 shorter events, 0.1 us)
Async XLA Ops:
  20.9 0.8 copy-start

commit v2 on v1

--- a/solution.py
+++ b/solution.py
@@ -372,7 +372,7 @@
             pltpu.VMEM((3 * edges, low), BF),
             pltpu.VMEM((blocks, edges, ch), F32),
         ],
-        compiler_params=pltpu.CompilerParams(vmem_limit_bytes=56 * 2**20),
+        compiler_params=pltpu.CompilerParams(vmem_limit_bytes=48 * 2**20),
     )(*args)
 
 
@@ -587,7 +587,7 @@
             pltpu.SemaphoreType.DMA((PARTS,)),
         ],
         compiler_params=pltpu.CompilerParams(
-            collective_id=1, has_side_effects=True, vmem_limit_bytes=56 * 2**20
+            collective_id=1, has_side_effects=True, vmem_limit_bytes=51 * 2**20
         ),
     )(terms.reshape(nz, nx, rows_padded, ch), node_terms)
 

time: 99.3 us -> 92.7 us (0.934)
  local copies, waits for them, and re-layouts: 14.3 us -> 10.7 us
  Pallas kernels: 82.4 us -> 79.3 us
    slice x3, local copies, waits for them, and re-layouts: 2.91 us -> 0.05 us  [per_device(): block = shard[at:at + rows * len(mine)].reshape(len(mine), rows, ch)]
    unnamed x4 -> x16, local copies, waits for them, and re-layouts: 2.46 us -> 5.27 us
    pallas_call x1, Pallas kernels: 52.6 us -> 50.7 us  [reduce_all(): pl.pallas_call(functools.partial(reduce_kernel, ny, nx, nz, h), name='red...]
    pallas_call x1, Pallas kernels: 15.5 us -> 14.2 us  [compute(): pl.pallas_call(functools.partial(compute_kernel, peers, nodes, slots, hea...]
where the time goes in v2:
time: 92.7 us; the launch traced here: 92.2 us
  Pallas kernels  79.3 us (86%)
  local copies, waits for them, and re-layouts  10.7 us (12%)
  between operations  1.57 us (2%)
    pallas_call x1, Pallas kernels, reduce_all(): pl.pallas_call(functools.partial(reduce_kernel, ny, nx, nz, h), name='red...  50.7 us
    pallas_call x1, Pallas kernels, gather_nodes(): pl.pallas_call(functools.partial(gather_kernel, nx, nz), name='gather_nod...  14.4 us
    pallas_call x1, Pallas kernels, compute(): pl.pallas_call(functools.partial(compute_kernel, peers, nodes, slots, hea...  14.2 us
    unnamed x16, local copies, waits for them, and re-layouts  5.27 us
    convert_element_type x7, local copies, waits for them, and re-layouts, per_device(): outs.append(block.transpose(1, 0, 2).reshape(rows, -1).astype(F32))  1.97 us

profile of v2, /device:TPU:0, one launch (start us, length us, event | category | flops | bytes accessed | tf_op | source)
XLA Modules:
  0.0 92.2 jit_solution(17508797161102905767)
XLA Ops:
  0.6 0.0 copy-start.6
  0.6 0.0 copy-start.5
  0.7 0.0 copy-start
  0.7 0.0 copy-start.4
  1.4 0.8 copy.37.req_ref
  2.2 0.8 pad.11
  3.0 0.8 pad.12
  3.9 0.9 copy.36
  4.8 14.4 %gather_nodes.1.g_ref = bf16[128,1664]{1,0:T(8,128)(2,1)S(1)} custom-call(bf16[16,1664]{1,0:T(8,128)(2,1)S(1)} %reshape.66.x_ref), custom_call_target="tpu_custom_call" | custom-call | tf_op jit(solution)/shard_map/gather_nodes/pallas_call | solution.py:104
  19.2 0.0 copy-done.6
  19.2 0.0 copy-done.5
  19.2 0.0 copy-done
  19.2 0.0 copy-done.4
  19.3 0.0 copy-start.1
  19.3 1.3 %copy-done.1 = bf16[768,768]{1,0:T(8,128)(2,1)S(1)} copy-done((bf16[768,768]{1,0:T(8,128)(2,1)S(1)}, bf16[768,768]{1,0:T(8,128)(2,1)}, u32[]{:S(2)}) %copy-start.1) | copy-done | bytes 1179672
  20.5 0.0 copy-start.2
  20.5 1.1 %copy-done.2 = bf16[640,640]{1,0:T(8,128)(2,1)S(1)} copy-done((bf16[640,640]{1,0:T(8,128)(2,1)S(1)}, bf16[640,640]{1,0:T(8,128)(2,1)}, u32[]{:S(2)}) %copy-start.2) | copy-done | bytes 819224
  21.7 0.0 copy-start.3
  21.7 1.1 %copy-done.3 = bf16[640,640]{1,0:T(8,128)(2,1)S(1)} copy-done((bf16[640,640]{1,0:T(8,128)(2,1)S(1)}, bf16[640,640]{1,0:T(8,128)(2,1)}, u32[]{:S(2)}) %copy-start.3) | copy-done | bytes 819224
  22.8 14.2 %edge_backward.1 = (bf16[8,2816,128]{2,1,0:T(8,128)(2,1)}, bf16[128,1664]{1,0:T(8,128)(2,1)S(1)}) custom-call(bf16[128,1664]{1,0:T(8,128)(2,1)S(1)} %gather_nodes.1.g_ref, bf16[16,1664]{1,0:T(8,128)(2,1)S(1)} %reshape.68.cot_ref, f32[235,128]{1,0:T(8,128)S(1)} %copy-done.4, bf16[896,896]{1,0:T(8,128)(2,1)} %wz_ref.1, bf16[768,768]{1,0:T(8,128)(2,1)S(1)} %copy-done, ...), custom_call_target="tpu_custom_call" | custom-call | tf_op jit(solution)/shard_map/edge_backward/pallas_call | solution.py:351
  37.0 50.7 %reduce_all.1 = (bf16[2816,128]{1,0:T(8,128)(2,1)S(1)}, f32[16,1664]{1,0:T(8,128)S(1)}) custom-call(bf16[4,2,2816,128]{3,2,1,0:T(8,128)(2,1)} %bitcast.46, bf16[128,1664]{1,0:T(8,128)(2,1)S(1)} %get-tuple-element.12.n_ref), custom_call_target="tpu_custom_call" | custom-call | tf_op jit(solution)/shard_map/reduce_all/pallas_call | solution.py:567
  87.7 0.6 slice.35
  88.4 0.1 fusion
  88.5 0.1 copy.43
  88.5 0.1 copy.44
  88.6 0.7 maximum_convert_fusion
  89.5 0.8 copy_bitcast_fusion.3
  90.3 0.1 copy.39
  90.3 0.1 copy.40
  90.4 0.9 copy_bitcast_fusion.1
  91.4 0.8 copy.55
  (10 shorter events, 0.3 us)
Async XLA Ops:
  0.6 18.6 %copy-start.6 = (s32[128]{0:T(128)S(1)}, s32[128]{0:T(128)}, u32[]{:S(2)}) copy-start(s32[128]{0:T(128)} %param.23) | copy-start | bytes 1540
  0.6 18.6 %copy-start.5 = (s32[128]{0:T(128)S(1)}, s32[128]{0:T(128)}, u32[]{:S(2)}) copy-start(s32[128]{0:T(128)} %param.22) | copy-start | bytes 1540
  0.7 18.6 %copy-start = (bf16[768,768]{1,0:T(8,128)(2,1)S(1)}, bf16[768,768]{1,0:T(8,128)(2,1)}, u32[]{:S(2)}) copy-start(bf16[768,768]{1,0:T(8,128)(2,1)} %w1r_ref.1) | copy-start | bytes 3538948
  0.7 18.6 %copy-start.4 = (f32[235,128]{1,0:T(8,128)S(1)}, f32[235,128]{1,0:T(8,128)}, u32[]{:S(2)}) copy-start(f32[235,128]{1,0:T(8,128)} %wig_ref.1) | copy-start | bytes 360964
  19.3 1.3 %copy-start.1 = (bf16[768,768]{1,0:T(8,128)(2,1)S(1)}, bf16[768,768]{1,0:T(8,128)(2,1)}, u32[]{:S(2)}) copy-start(bf16[768,768]{1,0:T(8,128)(2,1)} %w1i_ref.1) | copy-start | bytes 3538948
  20.5 1.1 %copy-start.2 = (bf16[640,640]{1,0:T(8,128)(2,1)S(1)}, bf16[640,640]{1,0:T(8,128)(2,1)}, u32[]{:S(2)}) copy-start(bf16[640,640]{1,0:T(8,128)(2,1)} %w2r_ref.1) | copy-start | bytes 2457604
  21.7 1.1 %copy-start.3 = (bf16[640,640]{1,0:T(8,128)(2,1)S(1)}, bf16[640,640]{1,0:T(8,128)(2,1)}, u32[]{:S(2)}) copy-start(bf16[640,640]{1,0:T(8,128)(2,1)} %w2i_ref.1) | copy-start | bytes 2457604
